TPU v7x, 256 devices: a whole 4x4x8 slice. The times are simulated.
256 devices in a mesh: leaf: 32 (over z, y), front: 8 (over x, core).
Axes of the slice: x: 4, y: 4, z: 8, core: 2. Of those that a mesh axis runs over, the one named last changes fastest.
Arguments:
- leaf_fronts: float32 [32, 1024, 1024], P('leaf', 'front')
- coupling_cols: int32 [32, 8, 124, 128], P('leaf', 'front'), may hold values from 0 to 1023, as said below
- coupling_vals: float32 [32, 8, 124, 128], P('leaf', 'front'), may hold values from -0.1 to 0.1
- sep_diag: float32 [32, 8, 124], P('leaf', 'front'), may hold values from 1 to 3
- child_maps: int32 [62, 512], replicated, may hold values from 0 to 1023, as said below
Outputs:
- factors: float32 [32, 8, 252, 512], P('leaf', 'front')
- log_det: float32 [], replicated
Inputs may be any that keep to these rules, and one draw needn't show every extreme that they name: `coupling_cols`: each coupling column is at most the index, in its front, of the row that holds it, so every entry lies on or below the diagonal. `child_maps`: the 512 entries of each row are distinct.
All inputs are finite; a program needn't handle non-finite values.
Results may differ from a plain program's by a relative error of at most 0.0001.
Values sent between devices are 32-bit elements; how exact they have to be, the bound alone decides.
A program may use at most 128 MiB of HBM per device.

v0:
```python
import jax
import jax.numpy as jnp
from jax import lax
from jax.sharding import PartitionSpec as P

SEP = 512
BND = 512
highest_precision = lax.Precision.HIGHEST


def swapped(block, axis, distance):
    count = lax.axis_size(axis)
    route = []
    for low in range(count):
        high = low | 1 << distance
        if high != low and high < count:
            route += [(low, high), (high, low)]
    return lax.ppermute(block, axis, route)


def from_behind(block, axis, distance):
    devices = range(lax.axis_size(axis))
    route = [(i - distance, i) for i in devices if i - distance in devices]
    return lax.ppermute(block, axis, route)


def symmetric_of(lower_tri):
    return lower_tri + lower_tri.T - jnp.diag(jnp.diag(lower_tri))


def double_up(gathered, partner, bit_pos):
    leaf_pos = lax.axis_index("leaf")
    high_side = leaf_pos >> bit_pos & 1 == 1
    first_half = jnp.where(high_side, partner, gathered)
    second_half = jnp.where(high_side, gathered, partner)
    return jnp.concatenate([first_half, second_half], axis=0)


def collect(strip_piece, bit_count, is_panel):
    if is_panel:
        gathered = lax.all_gather(strip_piece, "front", axis=0, tiled=True)
    else:
        gathered = lax.all_gather(strip_piece, "front", axis=0, tiled=True)
    for bit_pos in range(bit_count):
        if is_panel:
            partner = swapped(gathered, "leaf", bit_pos)
        else:
            partner = swapped(gathered, "leaf", bit_pos)
        gathered = double_up(gathered, partner, bit_pos)
    return gathered


def twin_order(gathered, group_size):
    row_count = gathered.shape[0] // (2 * group_size)
    col_count = gathered.shape[1]
    arranged = gathered.reshape(2, 2, group_size // 2, row_count, col_count)
    return arranged.transpose(0, 2, 1, 3, 4).reshape(2, group_size * row_count, col_count)


def child_rows(update_rows, index_map, row_ids):
    match_grid = index_map[None, :] == row_ids[:, None]
    child_ids = jnp.arange(index_map.shape[0], dtype=jnp.int32)
    present = jnp.any(match_grid, axis=1)
    source = jnp.sum(jnp.where(match_grid, child_ids[None, :], 0), axis=1)
    row_part = jnp.take(update_rows, source, axis=0)
    col_part = jnp.take(update_rows, source, axis=1).T
    picked = jnp.where(child_ids[None, :] <= source[:, None], row_part, col_part)
    return jnp.where(present[:, None], picked, 0.0)


def body(leaf_fronts, coupling_cols, coupling_vals, sep_diag, child_maps):
    group_count = lax.axis_size("leaf")
    front_count = lax.axis_size("front")
    level_total = group_count.bit_length()
    width_all = SEP + BND
    leaf_pos = lax.axis_index("leaf")
    front_pos = lax.axis_index("front")
    size_rows = width_all // front_count
    row_ids = front_pos * size_rows + jnp.arange(size_rows, dtype=jnp.int32)
    column_ids = jnp.arange(width_all, dtype=jnp.int32)
    front_strip = jnp.where(column_ids[None, :] <= row_ids[:, None], leaf_fronts[0], 0.0)
    pieces_out = []
    log_part = jnp.zeros((), jnp.float32)
    list_offset = 0
    map_base = 0
    for level_no in range(level_total):
        span_leaf = 1 << level_no
        size_rows = width_all // (front_count * span_leaf)
        group_rank = (leaf_pos & span_leaf - 1) * front_count + front_pos
        start_row = group_rank * size_rows
        panel_piece = front_strip[:, :SEP]
        panel_cols = collect(panel_piece, level_no, True)
        head_block = symmetric_of(panel_cols[:SEP])
        chol_head = jnp.linalg.cholesky(head_block)
        below = jax.scipy.linalg.solve_triangular(chol_head, panel_cols[SEP:].T, lower=True).T
        factor_cols = jnp.concatenate([chol_head, below], axis=0)
        pieces_out.append(lax.dynamic_slice_in_dim(factor_cols, start_row, size_rows, 0))
        head_diag = jnp.diagonal(chol_head)
        owned_rows = jnp.arange(SEP, dtype=jnp.int32) // size_rows == group_rank
        log_part = log_part + jnp.sum(jnp.where(owned_rows, jnp.log(head_diag), 0.0))
        if level_no + 1 < level_total:
            group_size = span_leaf * front_count
            half_rows = size_rows // 2
            holds_tail = group_rank >= group_size // 2
            update_start = start_row - jnp.where(holds_tail, SEP, 0)
            tail_rows = front_strip[:, SEP:]

            def tail_term():
                own_below = lax.dynamic_slice_in_dim(
                    below, jnp.clip(update_start, 0, BND - size_rows), size_rows, 0
                )
                return tail_rows - jnp.dot(
                    own_below,
                    below.T,
                    precision=highest_precision,
                    preferred_element_type=jnp.float32,
                )

            def empty_term():
                return jnp.zeros((size_rows, BND), jnp.float32)

            difference = lax.cond(holds_tail, tail_term, empty_term)
            leading = difference[:half_rows]
            if level_no == 0:
                received = from_behind(leading, "front", -(front_count // 2))
            else:
                received = from_behind(leading, "leaf", -(1 << level_no - 1))
            outgoing = jnp.where(holds_tail, difference[half_rows:], received)
            gathered = twin_order(collect(outgoing, level_no + 1, False), group_size)
            parent_span = span_leaf * 2
            next_rows = width_all // (front_count * parent_span)
            parent_rank = (leaf_pos & parent_span - 1) * front_count + front_pos
            row_ids = parent_rank * next_rows + jnp.arange(next_rows, dtype=jnp.int32)
            parent_no = leaf_pos >> level_no + 1
            assembled = jnp.zeros((next_rows, width_all), jnp.float32)
            for child_no in range(2):
                index_map = lax.dynamic_slice_in_dim(
                    child_maps, map_base + 2 * parent_no + child_no, 1, 0
                )[0]
                picked = child_rows(gathered[child_no], index_map, row_ids)
                assembled = assembled.at[:, index_map].add(picked)
            assembled = jnp.where(column_ids[None, :] <= row_ids[:, None], assembled, 0.0)
            col_block = coupling_cols[0, 0, list_offset : list_offset + next_rows, :]
            val_block = coupling_vals[0, 0, list_offset : list_offset + next_rows, :]
            local_rows = jnp.arange(next_rows, dtype=jnp.int32)
            assembled = assembled.at[local_rows[:, None], col_block].add(val_block)
            diag_piece = sep_diag[0, 0, list_offset : list_offset + next_rows]
            assembled = assembled + jnp.where(
                column_ids[None, :] == row_ids[:, None], diag_piece[:, None], 0.0
            )
            front_strip = assembled
            list_offset = list_offset + next_rows
            map_base = map_base + group_count // span_leaf
    log_det = 2.0 * lax.psum(log_part, ("leaf", "front"))
    factors = jnp.concatenate(pieces_out, axis=0)[None, None]
    return (factors, log_det)


def solution(mesh):
    placed = (
        P("leaf", "front", None),
        P("leaf", "front", None, None),
        P("leaf", "front", None, None),
        P("leaf", "front", None),
        P(),
    )
    return jax.shard_map(
        body,
        mesh=mesh,
        in_specs=placed,
        out_specs=(P("leaf", "front", None, None), P()),
        check_vma=False,
    )
```

profile of v0, /device:TPU:1, one launch (start us, length us, event | category | flops | bytes accessed | tf_op | source)
XLA Modules:
  0.0 2185.0 jit_solution(17562657626396560996)
XLA Ops:
  9.3 33.1 %all-gather.6.cloned.1.call-done = f32[1024,512]{1,0:T(8,128)} async-done(((f32[128,512]{1,0:T(8,128)}), f32[1024,512]{1,0:T(8,128)}) %all-gather.6.cloned.1.call-update) | async-done | bytes 2097168 | tf_op jit(solution)/shard_map/all_gather | solution.py:41
  52.0 11.7 cholesky.638
  76.2 11.7 cholesky.657
  99.5 11.7 cholesky.678
  140.5 12.0 while.12
  152.5 39.3 %custom-call.72 = f32[4,128,128]{1,2,0:T(8,128)S(1)} custom-call(f32[4,128,128]{2,1,0:T(8,128)S(1)} %get-tuple-element.167), custom_call_target="InvertDiagBlocksLowerTriangular" | custom-call | tf_op jit(solution)/shard_map/jit(_solve_triangular)/triangular_solve | solution.py:95
  215.7 23.5 %all-gather.8.cloned.1.call-done = f32[512,512]{1,0:T(8,128)} async-done(((f32[64,512]{1,0:T(8,128)}), f32[512,512]{1,0:T(8,128)}) %all-gather.8.cloned.1.call-update) | async-done | bytes 1048592 | tf_op jit(solution)/shard_map/all_gather | solution.py:43
  243.6 20.4 collective-permute-done.1
  278.8 57.0 %scatter_fusion.6 = f32[65536]{0:T(1024)S(1)} fusion(f32[65536]{0:T(1024)S(1)} %bitcast.497, s32[8192]{0:T(1024)S(1)} %copy-done.34, f32[8192]{0:T(1024)S(1)} %bitcast.526), kind=kCustom, calls=%fused_computation.43 | custom fusion | flops 8192 | bytes 131072
  336.7 26.7 %all-gather.10.cloned.1.call-done = f32[512,512]{1,0:T(8,128)} async-done(((f32[64,512]{1,0:T(8,128)}), f32[512,512]{1,0:T(8,128)}) %all-gather.10.cloned.1.call-update) | async-done | bytes 1048592 | tf_op jit(solution)/shard_map/all_gather | solution.py:41
  365.8 22.4 %collective-permute-done.2 = f32[512,512]{1,0:T(8,128)S(1)} collective-permute-done((f32[512,512]{1,0:T(8,128)}, f32[512,512]{1,0:T(8,128)S(1)}, u32[]{:S(2)}, u32[]{:S(2)}) %collective-permute-start.2) | collective-permute-done | bytes 1048608 | tf_op jit(solution)/shard_map/ppermute | solution.py:18
  472.3 12.1 cholesky.767
  500.6 39.9 %custom-call.76 = f32[4,128,128]{1,2,0:T(8,128)} custom-call(f32[4,128,128]{2,1,0:T(8,128)S(1)} %get-tuple-element.168), custom_call_target="InvertDiagBlocksLowerTriangular" | custom-call | tf_op jit(solution)/shard_map/jit(_solve_triangular)/triangular_solve | solution.py:95
  567.6 14.9 all_gather.36
  602.7 22.6 %collective-permute-done.5 = f32[512,512]{1,0:T(8,128)} collective-permute-done((f32[512,512]{1,0:T(8,128)}, f32[512,512]{1,0:T(8,128)}, u32[]{:S(2)}, u32[]{:S(2)}) %collective-permute-start.5) | collective-permute-done | bytes 1048608 | tf_op jit(solution)/shard_map/ppermute | solution.py:18
  647.6 28.8 %scatter_fusion.7 = f32[32768]{0:T(1024)S(1)} fusion(f32[32768]{0:T(1024)S(1)} %bitcast.498, s32[4096]{0:T(1024)S(1)} %select_bitcast_fusion.24, f32[4096]{0:T(1024)S(1)} %bitcast.527), kind=kCustom, calls=%fused_computation.44 | custom fusion | flops 4096 | bytes 65536
  676.5 14.3 all_gather.37
  691.4 12.7 collective-permute-done.6
  708.2 22.3 %collective-permute-done.7 = f32[512,512]{1,0:T(8,128)} collective-permute-done((f32[512,512]{1,0:T(8,128)S(1)}, f32[512,512]{1,0:T(8,128)}, u32[]{:S(2)}, u32[]{:S(2)}) %collective-permute-start.7) | collective-permute-done | bytes 1048608 | tf_op jit(solution)/shard_map/ppermute | solution.py:18
  772.6 12.5 cholesky.801
  822.7 11.9 cholesky.839
  839.4 11.7 while.14
  851.2 39.9 %custom-call.80 = f32[4,128,128]{1,2,0:T(8,128)} custom-call(f32[4,128,128]{2,1,0:T(8,128)S(1)} %get-tuple-element.169), custom_call_target="InvertDiagBlocksLowerTriangular" | custom-call | tf_op jit(solution)/shard_map/jit(_solve_triangular)/triangular_solve | solution.py:95
  919.4 15.4 all_gather.38
  961.3 21.7 collective-permute-done.11
  1005.2 14.7 scatter_fusion.8
  1019.9 15.2 all_gather.39
  1059.3 21.6 collective-permute-done.14
  1122.5 11.7 cholesky.873
  1170.1 11.9 cholesky.911
  1198.1 39.9 %custom-call.84 = f32[4,128,128]{1,2,0:T(8,128)} custom-call(f32[4,128,128]{2,1,0:T(8,128)S(1)} %get-tuple-element.170), custom_call_target="InvertDiagBlocksLowerTriangular" | custom-call | tf_op jit(solution)/shard_map/jit(_solve_triangular)/triangular_solve | solution.py:95
  1264.3 16.2 all_gather.40
  1314.1 45.0 %collective-permute-done.19 = f32[512,512]{1,0:T(8,128)} collective-permute-done((f32[512,512]{1,0:T(8,128)}, f32[512,512]{1,0:T(8,128)}, u32[]{:S(2)}, u32[]{:S(2)}) %collective-permute-start.19) | collective-permute-done | bytes 1048608 | tf_op jit(solution)/shard_map/ppermute | solution.py:18
  1388.9 14.0 all_gather.41
  1431.5 45.2 %collective-permute-done.23 = f32[512,512]{1,0:T(8,128)} collective-permute-done((f32[512,512]{1,0:T(8,128)S(1)}, f32[512,512]{1,0:T(8,128)}, u32[]{:S(2)}, u32[]{:S(2)}) %collective-permute-start.23) | collective-permute-done | bytes 1048608 | tf_op jit(solution)/shard_map/ppermute | solution.py:18
  1518.1 11.7 cholesky.945
  1565.7 12.1 cholesky.983
  1594.0 39.9 %custom-call.88 = f32[4,128,128]{1,2,0:T(8,128)} custom-call(f32[4,128,128]{2,1,0:T(8,128)S(1)} %get-tuple-element.171), custom_call_target="InvertDiagBlocksLowerTriangular" | custom-call | tf_op jit(solution)/shard_map/jit(_solve_triangular)/triangular_solve | solution.py:95
  1659.4 15.1 all-gather
  1695.8 22.6 %collective-permute-done.28 = f32[256,512]{1,0:T(8,128)} collective-permute-done((f32[256,512]{1,0:T(8,128)S(1)}, f32[256,512]{1,0:T(8,128)}, u32[]{:S(2)}, u32[]{:S(2)}) %collective-permute-start.28) | collective-permute-done | bytes 524320 | tf_op jit(solution)/shard_map/ppermute | solution.py:18
  1722.7 47.7 %collective-permute-done.29 = f32[512,512]{1,0:T(8,128)} collective-permute-done((f32[512,512]{1,0:T(8,128)}, f32[512,512]{1,0:T(8,128)}, u32[]{:S(2)}, u32[]{:S(2)}) %collective-permute-start.29) | collective-permute-done | bytes 1048608 | tf_op jit(solution)/shard_map/ppermute | solution.py:18
  1801.1 24.8 %scatter_fusion.5 = f32[4,1024]{1,0:T(4,128)S(1)} fusion(f32[4,1024]{1,0:T(4,128)S(1)} %add.625, s32[512]{0:T(512)S(1)} %fusion.262, f32[512]{0:T(512)S(1)} %bitcast.530), kind=kCustom, calls=%fused_computation.42 | custom fusion | flops 512 | bytes 10240 | tf_op jit(solution)/shard_map/scatter-add | solution.py:146
  1826.0 13.6 all-gather.1
  1861.9 18.8 collective-permute-done.33
  1913.9 20.8 collective-permute-done.34
  2012.2 11.9 cholesky.1055
  2040.2 39.3 %custom-call.92 = f32[4,128,128]{1,2,0:T(8,128)S(1)} custom-call(f32[4,128,128]{2,1,0:T(8,128)S(1)} %get-tuple-element.172), custom_call_target="InvertDiagBlocksLowerTriangular" | custom-call | tf_op jit(solution)/shard_map/jit(_solve_triangular)/triangular_solve | solution.py:95
  2095.1 76.0 %psum.7 = f32[]{:T(128)} all-reduce(f32[]{:T(128)S(6)} %add.634), channel_id=1, replica_groups=mesh['leaf'=32,'front'=8] {'leaf','front'}, use_global_device_ids=true, to_apply=%region_59.72 | all-reduce | flops 1 | bytes 8 | tf_op jit(solution)/shard_map/psum | solution.py:154
  (807 shorter events, 1075.6 us)
Async XLA Ops:
  7.2 35.2 %all-gather.6.cloned.1.call-start = ((), (), s32[]{:S(2)}) async-start(), calls=%async_computation | async-start | bytes 2359296 | tf_op jit(solution)/shard_map/all_gather | solution.py:41
  9.2 230.0 %all-gather.8.cloned.1.call-start = ((), (), s32[]{:S(2)}) async-start(), calls=%async_computation.1 | async-start | bytes 1179648 | tf_op jit(solution)/shard_map/all_gather | solution.py:43
  204.2 37.7 %copy-start.63 = (f32[1,1,124]{2,1,0:T(1,128)S(1)}, f32[1,1,124]{2,1,0:T(1,128)}, u32[]{:S(2)}) copy-start(f32[1,1,124]{2,1,0:T(1,128)} %param.41) | copy-start | bytes 1492
  204.3 8.8 collective-permute-start
  213.7 149.7 %all-gather.10.cloned.1.call-start = ((), (), s32[]{:S(2)}) async-start(), calls=%async_computation.2 | async-start | bytes 1179648 | tf_op jit(solution)/shard_map/all_gather | solution.py:41
  213.8 51.6 %copy-start.54 = (s32[64]{0:T(128)}, s32[64]{0:T(128)S(1)}, u32[]{:S(2)}) copy-start(s32[64]{0:T(128)S(1)} %iota_add_fusion.4) | copy-start | bytes 772
  215.7 49.8 %copy-start.51 = (s32[64]{0:T(128)}, s32[64]{0:T(128)S(1)}, u32[]{:S(2)}) copy-start(s32[64]{0:T(128)S(1)} %get-tuple-element.300) | copy-start | bytes 772
  239.2 24.7 %collective-permute-start.1 = (f32[512,512]{1,0:T(8,128)}, f32[512,512]{1,0:T(8,128)S(1)}, u32[]{:S(2)}, u32[]{:S(2)}) collective-permute-start(f32[512,512]{1,0:T(8,128)} %all-gather.8.cloned.1.call-done), channel_id=1, source_target_pairs={{0,8},{8,0},{16,24},{24,16},{32,40},{40,32},{48,56},{56,48},{64,72... | collective-permute-start | bytes 3145736 | tf_op jit(solution)/shard_map/ppermute | solution.py:18
  278.8 85.8 %copy-start.35 = (s32[1,1,124,128]{3,1,2,0:T(1,128)S(1)}, s32[1,1,124,128]{3,1,2,0:T(1,128)}, u32[]{:S(2)}) copy-start(s32[1,1,124,128]{3,1,2,0:T(1,128)} %param.39) | copy-start | bytes 190468
  363.4 24.7 %collective-permute-start.2 = (f32[512,512]{1,0:T(8,128)}, f32[512,512]{1,0:T(8,128)S(1)}, u32[]{:S(2)}, u32[]{:S(2)}) collective-permute-start(f32[512,512]{1,0:T(8,128)} %all-gather.10.cloned.1.call-done), channel_id=1, source_target_pairs={{0,8},{8,0},{16,24},{24,16},{32,40},{40,32},{48,56},{56,48},{64,72... | collective-permute-start | bytes 3145736 | tf_op jit(solution)/shard_map/ppermute | solution.py:18
  488.9 55.3 %copy-start.16 = (f32[512,512]{0,1:T(8,128)S(1)}, f32[512,512]{0,1:T(8,128)}, u32[]{:S(2)}) copy-start(f32[512,512]{0,1:T(8,128)} %get-tuple-element.418) | copy-start | bytes 3145732
  560.8 6.8 collective-permute-start.3
  582.4 14.0 collective-permute-start.4
  597.6 27.7 %collective-permute-start.5 = (f32[512,512]{1,0:T(8,128)}, f32[512,512]{1,0:T(8,128)}, u32[]{:S(2)}, u32[]{:S(2)}) collective-permute-start(f32[512,512]{1,0:T(8,128)} %pad_maximum_fusion.7), channel_id=1, source_target_pairs={{0,16},{16,0},{8,24},{24,8},{32,48},{48,32},{40,56},{56,40},{64,80... | collective-permute-start | bytes 3145736 | tf_op jit(solution)/shard_map/ppermute | solution.py:18
  690.8 13.4 collective-permute-start.6
  705.2 25.3 %collective-permute-start.7 = (f32[512,512]{1,0:T(8,128)S(1)}, f32[512,512]{1,0:T(8,128)}, u32[]{:S(2)}, u32[]{:S(2)}) collective-permute-start(f32[512,512]{1,0:T(8,128)S(1)} %pad_maximum_fusion.8), channel_id=1, source_target_pairs={{0,16},{16,0},{8,24},{24,8},{32,48},{48,32},{40,56},{56,40},{64,80... | collective-permute-start | bytes 3145736 | tf_op jit(solution)/shard_map/ppermute | solution.py:18
  839.4 55.4 %copy-start.13 = (f32[512,512]{0,1:T(8,128)S(1)}, f32[512,512]{0,1:T(8,128)}, u32[]{:S(2)}) copy-start(f32[512,512]{0,1:T(8,128)} %get-tuple-element.411) | copy-start | bytes 3145732
  911.3 8.1 collective-permute-start.8
  934.8 7.8 collective-permute-start.9
  942.7 15.5 collective-permute-start.10
  959.4 23.6 %collective-permute-start.11 = (f32[512,512]{1,0:T(8,128)}, f32[512,512]{1,0:T(8,128)}, u32[]{:S(2)}, u32[]{:S(2)}) collective-permute-start(f32[512,512]{1,0:T(8,128)} %pad_maximum_fusion.10), channel_id=1, source_target_pairs={{0,32},{32,0},{8,40},{40,8},{16,48},{48,16},{24,56},{56,24},{64,96... | collective-permute-start | bytes 3145736 | tf_op jit(solution)/shard_map/ppermute | solution.py:18
  1035.1 7.8 collective-permute-start.12
  1042.9 14.0 collective-permute-start.13
  1058.1 22.9 %collective-permute-start.14 = (f32[512,512]{1,0:T(8,128)S(1)}, f32[512,512]{1,0:T(8,128)}, u32[]{:S(2)}, u32[]{:S(2)}) collective-permute-start(f32[512,512]{1,0:T(8,128)S(1)} %pad_maximum_fusion.11), channel_id=1, source_target_pairs={{0,32},{32,0},{8,40},{40,8},{16,48},{48,16},{24,56},{56,24},{64,96... | collective-permute-start | bytes 3145736 | tf_op jit(solution)/shard_map/ppermute | solution.py:18
  1186.9 54.9 %copy-start.14 = (f32[512,512]{0,1:T(8,128)S(1)}, f32[512,512]{0,1:T(8,128)}, u32[]{:S(2)}) copy-start(f32[512,512]{0,1:T(8,128)} %get-tuple-element.405) | copy-start | bytes 3145732
  1258.2 6.1 collective-permute-start.15
  1280.6 4.9 collective-permute-start.16
  1285.6 8.4 collective-permute-start.17
  1294.1 12.2 collective-permute-start.18
  1307.4 51.7 %collective-permute-start.19 = (f32[512,512]{1,0:T(8,128)}, f32[512,512]{1,0:T(8,128)}, u32[]{:S(2)}, u32[]{:S(2)}) collective-permute-start(f32[512,512]{1,0:T(8,128)} %pad_maximum_fusion.13), channel_id=1, source_target_pairs={{0,64},{64,0},{8,72},{72,8},{16,80},{80,16},{24,88},{88,24},{32,96... | collective-permute-start | bytes 3145736 | tf_op jit(solution)/shard_map/ppermute | solution.py:18
  1402.9 4.9 collective-permute-start.20
  1407.9 8.4 collective-permute-start.21
  1416.4 11.6 collective-permute-start.22
  1429.1 47.6 %collective-permute-start.23 = (f32[512,512]{1,0:T(8,128)S(1)}, f32[512,512]{1,0:T(8,128)}, u32[]{:S(2)}, u32[]{:S(2)}) collective-permute-start(f32[512,512]{1,0:T(8,128)S(1)} %pad_maximum_fusion.14), channel_id=1, source_target_pairs={{0,64},{64,0},{8,72},{72,8},{16,80},{80,16},{24,88},{88,24},{32,96... | collective-permute-start | bytes 3145736 | tf_op jit(solution)/shard_map/ppermute | solution.py:18
  1582.8 54.9 %copy-start.15 = (f32[512,512]{0,1:T(8,128)S(1)}, f32[512,512]{0,1:T(8,128)}, u32[]{:S(2)}) copy-start(f32[512,512]{0,1:T(8,128)} %get-tuple-element.399) | copy-start | bytes 3145732
  1654.1 41.5 %copy-start.36 = (s32[1,512]{1,0:T(1,128)S(1)}, s32[1,512]{1,0:T(1,128)}, u32[]{:S(2)}) copy-start(s32[1,512]{1,0:T(1,128)} %get-tuple-element.490) | copy-start | bytes 6148
  1654.1 5.3 collective-permute-start.24
  1674.6 3.6 collective-permute-start.25
  1678.2 5.4 collective-permute-start.26
  1683.6 7.2 collective-permute-start.27
  1691.6 26.7 %collective-permute-start.28 = (f32[256,512]{1,0:T(8,128)S(1)}, f32[256,512]{1,0:T(8,128)}, u32[]{:S(2)}, u32[]{:S(2)}) collective-permute-start(f32[256,512]{1,0:T(8,128)S(1)} %pad_maximum_fusion.22), channel_id=1, source_target_pairs={{0,64},{64,0},{8,72},{72,8},{16,80},{80,16},{24,88},{88,24},{32,96... | collective-permute-start | bytes 1572872 | tf_op jit(solution)/shard_map/ppermute | solution.py:18
  1720.6 49.7 %collective-permute-start.29 = (f32[512,512]{1,0:T(8,128)}, f32[512,512]{1,0:T(8,128)}, u32[]{:S(2)}, u32[]{:S(2)}) collective-permute-start(f32[512,512]{1,0:T(8,128)} %pad_maximum_fusion.16), channel_id=1, source_target_pairs={{0,128},{128,0},{8,136},{136,8},{16,144},{144,16},{24,152},{152,24... | collective-permute-start | bytes 3145736 | tf_op jit(solution)/shard_map/ppermute | solution.py:18
  1839.6 3.6 collective-permute-start.30
  1843.2 5.4 collective-permute-start.31
  1848.7 5.7 collective-permute-start.32
  1855.2 25.5 %collective-permute-start.33 = (f32[256,512]{1,0:T(8,128)S(1)}, f32[256,512]{1,0:T(8,128)}, u32[]{:S(2)}, u32[]{:S(2)}) collective-permute-start(f32[256,512]{1,0:T(8,128)S(1)} %pad_maximum_fusion.23), channel_id=1, source_target_pairs={{0,64},{64,0},{8,72},{72,8},{16,80},{80,16},{24,88},{88,24},{32,96... | collective-permute-start | bytes 1572872 | tf_op jit(solution)/shard_map/ppermute | solution.py:18
  1883.1 51.6 %collective-permute-start.34 = (f32[512,512]{1,0:T(8,128)}, f32[512,512]{1,0:T(8,128)}, u32[]{:S(2)}, u32[]{:S(2)}) collective-permute-start(f32[512,512]{1,0:T(8,128)} %pad_maximum_fusion.17), channel_id=1, source_target_pairs={{0,128},{128,0},{8,136},{136,8},{16,144},{144,16},{24,152},{152,24... | collective-permute-start | bytes 3145736 | tf_op jit(solution)/shard_map/ppermute | solution.py:18
  2027.3 52.2 %copy-start.12 = (f32[512,512]{0,1:T(8,128)S(1)}, f32[512,512]{0,1:T(8,128)}, u32[]{:S(2)}) copy-start(f32[512,512]{0,1:T(8,128)} %get-tuple-element.393) | copy-start | bytes 3145732
  (66 other events, 648.0 us)
Sparse Core Ops, SparseCore 0:
  10.4 31.8 all-gather.5
  213.9 25.3 all-gather.7
  336.8 26.5 all-gather.9
where the time goes:
time: 2200 us; the launch traced here: 2180 us
  other arithmetic  971 us (44%)
  waiting for transfers between devices  565 us (26%)
  local copies, waits for them, and re-layouts  249 us (11%)
  blocking collectives  195 us (9%)
  matrix products  98.3 us (4%)
  starting transfers between devices  68.1 us (3%)
  between operations  37.8 us (2%)
    another operation x89, other arithmetic, body(): chol_head = jnp.linalg.cholesky(head_block)  479 us
    ppermute x30, waiting for transfers between devices, swapped(): return lax.ppermute(block, axis, route)  454 us
    another operation x18, other arithmetic, body(): jax.scipy.linalg.solve_triangular(chol_head, panel_cols[SEP:].T, lower=True)  258 us
    all_gather x8, blocking collectives, collect(): gathered = lax.all_gather(strip_piece, 'front', axis=0, tiled=True)  119 us
    unnamed x22, other arithmetic  113 us
    another operation x97, local copies, waits for them, and re-layouts, body(): jax.scipy.linalg.solve_triangular(chol_head, panel_cols[SEP:].T, lower=True)  89.5 us
    all_gather x3, waiting for transfers between devices, collect(): gathered = lax.all_gather(strip_piece, 'front', axis=0, tiled=True)  83.3 us
    psum x1, blocking collectives, body(): log_det = 2.0 * lax.psum(log_part, ('leaf', 'front'))  76 us
  transfers between devices with their start and end apart: 38, of which 38 were waited for; matrix products, arithmetic and copies ran while one was open for 2% of the time, Pallas kernels for 0%

commit v1 on v0

--- a/solution.py
+++ b/solution.py
@@ -151,7 +151,7 @@
             front_strip = assembled
             list_offset = list_offset + next_rows
             map_base = map_base + group_count // span_leaf
-    log_det = 2.0 * lax.psum(log_part, ("leaf", "front"))
+    log_det = 2.0 * lax.psum(lax.psum(log_part, "front"), "leaf")
     factors = jnp.concatenate(pieces_out, axis=0)[None, None]
     return (factors, log_det)
 

time: 2200 us -> 2210 us (level)
    psum x1 -> x2, blocking collectives: 76 us -> 74.6 us  [body(): log_det = 2.0 * lax.psum(lax.psum(log_part, 'front'), 'leaf')]
where the time goes in v1:
time: 2210 us; the launch traced here: 2180 us
  other arithmetic  971 us (44%)
  waiting for transfers between devices  565 us (26%)
  local copies, waits for them, and re-layouts  247 us (11%)
  blocking collectives  193 us (9%)
  matrix products  94.7 us (4%)
  starting transfers between devices  68.2 us (3%)
  between operations  37.8 us (2%)
    another operation x89, other arithmetic, body(): chol_head = jnp.linalg.cholesky(head_block)  479 us
    ppermute x30, waiting for transfers between devices, swapped(): return lax.ppermute(block, axis, route)  454 us
    another operation x18, other arithmetic, body(): jax.scipy.linalg.solve_triangular(chol_head, panel_cols[SEP:].T, lower=True)  258 us
    all_gather x8, blocking collectives, collect(): gathered = lax.all_gather(strip_piece, 'front', axis=0, tiled=True)  119 us
    unnamed x22, other arithmetic  113 us
    another operation x97, local copies, waits for them, and re-layouts, body(): jax.scipy.linalg.solve_triangular(chol_head, panel_cols[SEP:].T, lower=True)  89 us
    all_gather x3, waiting for transfers between devices, collect(): gathered = lax.all_gather(strip_piece, 'front', axis=0, tiled=True)  83.3 us
    psum x2, blocking collectives, body(): log_det = 2.0 * lax.psum(lax.psum(log_part, 'front'), 'leaf')  74.6 us
  transfers between devices with their start and end apart: 38, of which 38 were waited for; matrix products, arithmetic and copies ran while one was open for 2% of the time, Pallas kernels for 0%

profile of v1, /device:TPU:1, one launch (start us, length us, event | category | flops | bytes accessed | tf_op | source)
XLA Modules:
  0.0 2177.4 jit_solution(17776904804176566811)
XLA Ops:
  9.3 33.1 %all-gather.6.cloned.1.call-done = f32[1024,512]{1,0:T(8,128)} async-done(((f32[128,512]{1,0:T(8,128)}), f32[1024,512]{1,0:T(8,128)}) %all-gather.6.cloned.1.call-update) | async-done | bytes 2097168 | tf_op jit(solution)/shard_map/all_gather | solution.py:41
  53.0 11.7 cholesky.638
  75.3 11.7 cholesky.657
  120.6 11.7 cholesky.695
  149.4 39.3 %custom-call.72 = f32[4,128,128]{1,2,0:T(8,128)S(1)} custom-call(f32[4,128,128]{2,1,0:T(8,128)S(1)} %get-tuple-element.167), custom_call_target="InvertDiagBlocksLowerTriangular" | custom-call | tf_op jit(solution)/shard_map/jit(_solve_triangular)/triangular_solve | solution.py:95
  212.6 23.5 %all-gather.8.cloned.1.call-done = f32[512,512]{1,0:T(8,128)} async-done(((f32[64,512]{1,0:T(8,128)}), f32[512,512]{1,0:T(8,128)}) %all-gather.8.cloned.1.call-update) | async-done | bytes 1048592 | tf_op jit(solution)/shard_map/all_gather | solution.py:43
  240.5 20.4 collective-permute-done.1
  275.7 57.0 %scatter_fusion.6 = f32[65536]{0:T(1024)S(1)} fusion(f32[65536]{0:T(1024)S(1)} %bitcast.497, s32[8192]{0:T(1024)S(1)} %copy-done.36, f32[8192]{0:T(1024)S(1)} %bitcast.526), kind=kCustom, calls=%fused_computation.43 | custom fusion | flops 8192 | bytes 131072
  333.6 26.7 %all-gather.10.cloned.1.call-done = f32[512,512]{1,0:T(8,128)} async-done(((f32[64,512]{1,0:T(8,128)}), f32[512,512]{1,0:T(8,128)}) %all-gather.10.cloned.1.call-update) | async-done | bytes 1048592 | tf_op jit(solution)/shard_map/all_gather | solution.py:41
  362.7 22.4 %collective-permute-done.2 = f32[512,512]{1,0:T(8,128)S(1)} collective-permute-done((f32[512,512]{1,0:T(8,128)}, f32[512,512]{1,0:T(8,128)S(1)}, u32[]{:S(2)}, u32[]{:S(2)}) %collective-permute-start.2) | collective-permute-done | bytes 1048608 | tf_op jit(solution)/shard_map/ppermute | solution.py:18
  469.2 12.1 cholesky.767
  497.5 39.9 %custom-call.76 = f32[4,128,128]{1,2,0:T(8,128)} custom-call(f32[4,128,128]{2,1,0:T(8,128)S(1)} %get-tuple-element.168), custom_call_target="InvertDiagBlocksLowerTriangular" | custom-call | tf_op jit(solution)/shard_map/jit(_solve_triangular)/triangular_solve | solution.py:95
  564.5 14.9 all_gather.36
  599.6 22.6 %collective-permute-done.5 = f32[512,512]{1,0:T(8,128)} collective-permute-done((f32[512,512]{1,0:T(8,128)}, f32[512,512]{1,0:T(8,128)}, u32[]{:S(2)}, u32[]{:S(2)}) %collective-permute-start.5) | collective-permute-done | bytes 1048608 | tf_op jit(solution)/shard_map/ppermute | solution.py:18
  644.5 28.8 %scatter_fusion.7 = f32[32768]{0:T(1024)S(1)} fusion(f32[32768]{0:T(1024)S(1)} %bitcast.498, s32[4096]{0:T(1024)S(1)} %select_bitcast_fusion.24, f32[4096]{0:T(1024)S(1)} %bitcast.527), kind=kCustom, calls=%fused_computation.44 | custom fusion | flops 4096 | bytes 65536
  673.4 14.3 all_gather.37
  688.3 12.7 collective-permute-done.6
  705.1 22.3 %collective-permute-done.7 = f32[512,512]{1,0:T(8,128)} collective-permute-done((f32[512,512]{1,0:T(8,128)S(1)}, f32[512,512]{1,0:T(8,128)}, u32[]{:S(2)}, u32[]{:S(2)}) %collective-permute-start.7) | collective-permute-done | bytes 1048608 | tf_op jit(solution)/shard_map/ppermute | solution.py:18
  769.5 12.5 cholesky.801
  819.6 11.9 cholesky.839
  836.3 11.7 while.14
  848.1 39.9 %custom-call.80 = f32[4,128,128]{1,2,0:T(8,128)} custom-call(f32[4,128,128]{2,1,0:T(8,128)S(1)} %get-tuple-element.169), custom_call_target="InvertDiagBlocksLowerTriangular" | custom-call | tf_op jit(solution)/shard_map/jit(_solve_triangular)/triangular_solve | solution.py:95
  916.3 15.4 all_gather.38
  958.2 21.7 collective-permute-done.11
  1002.1 14.7 scatter_fusion.8
  1016.8 15.2 all_gather.39
  1056.2 21.6 collective-permute-done.14
  1119.4 11.7 cholesky.873
  1167.0 11.9 cholesky.911
  1195.0 39.9 %custom-call.84 = f32[4,128,128]{1,2,0:T(8,128)} custom-call(f32[4,128,128]{2,1,0:T(8,128)S(1)} %get-tuple-element.170), custom_call_target="InvertDiagBlocksLowerTriangular" | custom-call | tf_op jit(solution)/shard_map/jit(_solve_triangular)/triangular_solve | solution.py:95
  1261.2 16.2 all_gather.40
  1311.0 45.0 %collective-permute-done.19 = f32[512,512]{1,0:T(8,128)} collective-permute-done((f32[512,512]{1,0:T(8,128)}, f32[512,512]{1,0:T(8,128)}, u32[]{:S(2)}, u32[]{:S(2)}) %collective-permute-start.19) | collective-permute-done | bytes 1048608 | tf_op jit(solution)/shard_map/ppermute | solution.py:18
  1385.8 14.0 all_gather.41
  1428.4 45.2 %collective-permute-done.23 = f32[512,512]{1,0:T(8,128)} collective-permute-done((f32[512,512]{1,0:T(8,128)S(1)}, f32[512,512]{1,0:T(8,128)}, u32[]{:S(2)}, u32[]{:S(2)}) %collective-permute-start.23) | collective-permute-done | bytes 1048608 | tf_op jit(solution)/shard_map/ppermute | solution.py:18
  1515.0 11.7 cholesky.945
  1562.6 12.1 cholesky.983
  1590.9 39.9 %custom-call.88 = f32[4,128,128]{1,2,0:T(8,128)} custom-call(f32[4,128,128]{2,1,0:T(8,128)S(1)} %get-tuple-element.171), custom_call_target="InvertDiagBlocksLowerTriangular" | custom-call | tf_op jit(solution)/shard_map/jit(_solve_triangular)/triangular_solve | solution.py:95
  1656.3 15.2 all-gather
  1692.0 22.5 %collective-permute-done.28 = f32[256,512]{1,0:T(8,128)} collective-permute-done((f32[256,512]{1,0:T(8,128)S(1)}, f32[256,512]{1,0:T(8,128)}, u32[]{:S(2)}, u32[]{:S(2)}) %collective-permute-start.28) | collective-permute-done | bytes 524320 | tf_op jit(solution)/shard_map/ppermute | solution.py:18
  1718.9 47.7 %collective-permute-done.29 = f32[512,512]{1,0:T(8,128)} collective-permute-done((f32[512,512]{1,0:T(8,128)}, f32[512,512]{1,0:T(8,128)}, u32[]{:S(2)}, u32[]{:S(2)}) %collective-permute-start.29) | collective-permute-done | bytes 1048608 | tf_op jit(solution)/shard_map/ppermute | solution.py:18
  1797.3 24.8 %scatter_fusion.5 = f32[4,1024]{1,0:T(4,128)S(1)} fusion(f32[4,1024]{1,0:T(4,128)S(1)} %add.627, s32[512]{0:T(512)S(1)} %fusion.262, f32[512]{0:T(512)S(1)} %bitcast.530), kind=kCustom, calls=%fused_computation.42 | custom fusion | flops 512 | bytes 10240 | tf_op jit(solution)/shard_map/scatter-add | solution.py:146
  1822.2 13.6 all-gather.1
  1857.4 18.8 collective-permute-done.33
  1909.4 20.8 collective-permute-done.34
  2007.7 11.9 cholesky.1055
  2035.7 39.3 %custom-call.92 = f32[4,128,128]{1,2,0:T(8,128)S(1)} custom-call(f32[4,128,128]{2,1,0:T(8,128)S(1)} %get-tuple-element.172), custom_call_target="InvertDiagBlocksLowerTriangular" | custom-call | tf_op jit(solution)/shard_map/jit(_solve_triangular)/triangular_solve | solution.py:95
  2086.1 12.7 psum.14
  2103.4 61.8 %psum.15 = f32[]{:T(128)} all-reduce(f32[]{:T(128)} %psum.14), channel_id=1, replica_groups=mesh['leaf'=32,'front'=8] {'leaf'}, use_global_device_ids=true, to_apply=%region_60.73 | all-reduce | flops 1 | bytes 8 | tf_op jit(solution)/shard_map/psum | solution.py:154
  (812 shorter events, 1081.0 us)
Async XLA Ops:
  7.2 35.2 %all-gather.6.cloned.1.call-start = ((), (), s32[]{:S(2)}) async-start(), calls=%async_computation | async-start | bytes 2359296 | tf_op jit(solution)/shard_map/all_gather | solution.py:41
  9.2 226.9 %all-gather.8.cloned.1.call-start = ((), (), s32[]{:S(2)}) async-start(), calls=%async_computation.1 | async-start | bytes 1179648 | tf_op jit(solution)/shard_map/all_gather | solution.py:43
  136.6 52.2 %copy-start.18 = (f32[512,512]{0,1:T(8,128)S(1)}, f32[512,512]{0,1:T(8,128)}, u32[]{:S(2)}) copy-start(f32[512,512]{0,1:T(8,128)} %get-tuple-element.423) | copy-start | bytes 3145732
  201.2 8.7 collective-permute-start
  210.6 149.7 %all-gather.10.cloned.1.call-start = ((), (), s32[]{:S(2)}) async-start(), calls=%async_computation.2 | async-start | bytes 1179648 | tf_op jit(solution)/shard_map/all_gather | solution.py:41
  210.7 51.7 %copy-start.56 = (s32[64]{0:T(128)}, s32[64]{0:T(128)S(1)}, u32[]{:S(2)}) copy-start(s32[64]{0:T(128)S(1)} %iota_add_fusion.4) | copy-start | bytes 772
  212.5 49.8 %copy-start.53 = (s32[64]{0:T(128)}, s32[64]{0:T(128)S(1)}, u32[]{:S(2)}) copy-start(s32[64]{0:T(128)S(1)} %get-tuple-element.300) | copy-start | bytes 772
  236.1 24.7 %collective-permute-start.1 = (f32[512,512]{1,0:T(8,128)}, f32[512,512]{1,0:T(8,128)S(1)}, u32[]{:S(2)}, u32[]{:S(2)}) collective-permute-start(f32[512,512]{1,0:T(8,128)} %all-gather.8.cloned.1.call-done), channel_id=1, source_target_pairs={{0,8},{8,0},{16,24},{24,16},{32,40},{40,32},{48,56},{56,48},{64,72... | collective-permute-start | bytes 3145736 | tf_op jit(solution)/shard_map/ppermute | solution.py:18
  275.7 85.8 %copy-start.37 = (s32[1,1,124,128]{3,1,2,0:T(1,128)S(1)}, s32[1,1,124,128]{3,1,2,0:T(1,128)}, u32[]{:S(2)}) copy-start(s32[1,1,124,128]{3,1,2,0:T(1,128)} %param.39) | copy-start | bytes 190468
  360.3 24.7 %collective-permute-start.2 = (f32[512,512]{1,0:T(8,128)}, f32[512,512]{1,0:T(8,128)S(1)}, u32[]{:S(2)}, u32[]{:S(2)}) collective-permute-start(f32[512,512]{1,0:T(8,128)} %all-gather.10.cloned.1.call-done), channel_id=1, source_target_pairs={{0,8},{8,0},{16,24},{24,16},{32,40},{40,32},{48,56},{56,48},{64,72... | collective-permute-start | bytes 3145736 | tf_op jit(solution)/shard_map/ppermute | solution.py:18
  485.8 55.3 %copy-start.17 = (f32[512,512]{0,1:T(8,128)S(1)}, f32[512,512]{0,1:T(8,128)}, u32[]{:S(2)}) copy-start(f32[512,512]{0,1:T(8,128)} %get-tuple-element.418) | copy-start | bytes 3145732
  557.7 6.8 collective-permute-start.3
  579.3 14.0 collective-permute-start.4
  594.5 27.7 %collective-permute-start.5 = (f32[512,512]{1,0:T(8,128)}, f32[512,512]{1,0:T(8,128)}, u32[]{:S(2)}, u32[]{:S(2)}) collective-permute-start(f32[512,512]{1,0:T(8,128)} %pad_maximum_fusion.7), channel_id=1, source_target_pairs={{0,16},{16,0},{8,24},{24,8},{32,48},{48,32},{40,56},{56,40},{64,80... | collective-permute-start | bytes 3145736 | tf_op jit(solution)/shard_map/ppermute | solution.py:18
  687.6 13.4 collective-permute-start.6
  702.1 25.3 %collective-permute-start.7 = (f32[512,512]{1,0:T(8,128)S(1)}, f32[512,512]{1,0:T(8,128)}, u32[]{:S(2)}, u32[]{:S(2)}) collective-permute-start(f32[512,512]{1,0:T(8,128)S(1)} %pad_maximum_fusion.8), channel_id=1, source_target_pairs={{0,16},{16,0},{8,24},{24,8},{32,48},{48,32},{40,56},{56,40},{64,80... | collective-permute-start | bytes 3145736 | tf_op jit(solution)/shard_map/ppermute | solution.py:18
  836.3 55.4 %copy-start.14 = (f32[512,512]{0,1:T(8,128)S(1)}, f32[512,512]{0,1:T(8,128)}, u32[]{:S(2)}) copy-start(f32[512,512]{0,1:T(8,128)} %get-tuple-element.411) | copy-start | bytes 3145732
  908.2 8.1 collective-permute-start.8
  931.7 7.8 collective-permute-start.9
  939.6 15.5 collective-permute-start.10
  956.3 23.6 %collective-permute-start.11 = (f32[512,512]{1,0:T(8,128)}, f32[512,512]{1,0:T(8,128)}, u32[]{:S(2)}, u32[]{:S(2)}) collective-permute-start(f32[512,512]{1,0:T(8,128)} %pad_maximum_fusion.10), channel_id=1, source_target_pairs={{0,32},{32,0},{8,40},{40,8},{16,48},{48,16},{24,56},{56,24},{64,96... | collective-permute-start | bytes 3145736 | tf_op jit(solution)/shard_map/ppermute | solution.py:18
  1032.0 7.8 collective-permute-start.12
  1039.8 14.0 collective-permute-start.13
  1055.0 22.9 %collective-permute-start.14 = (f32[512,512]{1,0:T(8,128)S(1)}, f32[512,512]{1,0:T(8,128)}, u32[]{:S(2)}, u32[]{:S(2)}) collective-permute-start(f32[512,512]{1,0:T(8,128)S(1)} %pad_maximum_fusion.11), channel_id=1, source_target_pairs={{0,32},{32,0},{8,40},{40,8},{16,48},{48,16},{24,56},{56,24},{64,96... | collective-permute-start | bytes 3145736 | tf_op jit(solution)/shard_map/ppermute | solution.py:18
  1183.7 54.9 %copy-start.15 = (f32[512,512]{0,1:T(8,128)S(1)}, f32[512,512]{0,1:T(8,128)}, u32[]{:S(2)}) copy-start(f32[512,512]{0,1:T(8,128)} %get-tuple-element.405) | copy-start | bytes 3145732
  1255.1 6.1 collective-permute-start.15
  1277.5 4.9 collective-permute-start.16
  1282.5 8.4 collective-permute-start.17
  1291.0 12.2 collective-permute-start.18
  1304.3 51.7 %collective-permute-start.19 = (f32[512,512]{1,0:T(8,128)}, f32[512,512]{1,0:T(8,128)}, u32[]{:S(2)}, u32[]{:S(2)}) collective-permute-start(f32[512,512]{1,0:T(8,128)} %pad_maximum_fusion.13), channel_id=1, source_target_pairs={{0,64},{64,0},{8,72},{72,8},{16,80},{80,16},{24,88},{88,24},{32,96... | collective-permute-start | bytes 3145736 | tf_op jit(solution)/shard_map/ppermute | solution.py:18
  1399.8 4.9 collective-permute-start.20
  1404.8 8.4 collective-permute-start.21
  1413.3 11.6 collective-permute-start.22
  1426.0 47.6 %collective-permute-start.23 = (f32[512,512]{1,0:T(8,128)S(1)}, f32[512,512]{1,0:T(8,128)}, u32[]{:S(2)}, u32[]{:S(2)}) collective-permute-start(f32[512,512]{1,0:T(8,128)S(1)} %pad_maximum_fusion.14), channel_id=1, source_target_pairs={{0,64},{64,0},{8,72},{72,8},{16,80},{80,16},{24,88},{88,24},{32,96... | collective-permute-start | bytes 3145736 | tf_op jit(solution)/shard_map/ppermute | solution.py:18
  1579.7 54.9 %copy-start.16 = (f32[512,512]{0,1:T(8,128)S(1)}, f32[512,512]{0,1:T(8,128)}, u32[]{:S(2)}) copy-start(f32[512,512]{0,1:T(8,128)} %get-tuple-element.399) | copy-start | bytes 3145732
  1651.0 5.3 collective-permute-start.24
  1671.5 3.6 collective-permute-start.25
  1675.1 5.4 collective-permute-start.26
  1680.6 7.2 collective-permute-start.27
  1687.9 26.7 %collective-permute-start.28 = (f32[256,512]{1,0:T(8,128)S(1)}, f32[256,512]{1,0:T(8,128)}, u32[]{:S(2)}, u32[]{:S(2)}) collective-permute-start(f32[256,512]{1,0:T(8,128)S(1)} %pad_maximum_fusion.22), channel_id=1, source_target_pairs={{0,64},{64,0},{8,72},{72,8},{16,80},{80,16},{24,88},{88,24},{32,96... | collective-permute-start | bytes 1572872 | tf_op jit(solution)/shard_map/ppermute | solution.py:18
  1716.9 49.7 %collective-permute-start.29 = (f32[512,512]{1,0:T(8,128)}, f32[512,512]{1,0:T(8,128)}, u32[]{:S(2)}, u32[]{:S(2)}) collective-permute-start(f32[512,512]{1,0:T(8,128)} %pad_maximum_fusion.16), channel_id=1, source_target_pairs={{0,128},{128,0},{8,136},{136,8},{16,144},{144,16},{24,152},{152,24... | collective-permute-start | bytes 3145736 | tf_op jit(solution)/shard_map/ppermute | solution.py:18
  1835.8 3.6 collective-permute-start.30
  1839.4 5.4 collective-permute-start.31
  1844.9 5.7 collective-permute-start.32
  1850.7 25.5 %collective-permute-start.33 = (f32[256,512]{1,0:T(8,128)S(1)}, f32[256,512]{1,0:T(8,128)}, u32[]{:S(2)}, u32[]{:S(2)}) collective-permute-start(f32[256,512]{1,0:T(8,128)S(1)} %pad_maximum_fusion.23), channel_id=1, source_target_pairs={{0,64},{64,0},{8,72},{72,8},{16,80},{80,16},{24,88},{88,24},{32,96... | collective-permute-start | bytes 1572872 | tf_op jit(solution)/shard_map/ppermute | solution.py:18
  1878.6 51.6 %collective-permute-start.34 = (f32[512,512]{1,0:T(8,128)}, f32[512,512]{1,0:T(8,128)}, u32[]{:S(2)}, u32[]{:S(2)}) collective-permute-start(f32[512,512]{1,0:T(8,128)} %pad_maximum_fusion.17), channel_id=1, source_target_pairs={{0,128},{128,0},{8,136},{136,8},{16,144},{144,16},{24,152},{152,24... | collective-permute-start | bytes 3145736 | tf_op jit(solution)/shard_map/ppermute | solution.py:18
  2022.8 52.2 %copy-start.13 = (f32[512,512]{0,1:T(8,128)S(1)}, f32[512,512]{0,1:T(8,128)}, u32[]{:S(2)}) copy-start(f32[512,512]{0,1:T(8,128)} %get-tuple-element.393) | copy-start | bytes 3145732
  2102.5 65.0 %copy-start.31 = (f32[252,512]{1,0:T(8,128)S(1)}, f32[252,512]{1,0:T(8,128)}, u32[]{:S(2)}) copy-start(f32[252,512]{1,0:T(8,128)} %fusion.244) | copy-start | bytes 1548292
  (68 other events, 745.5 us)
Sparse Core Ops, SparseCore 0:
  10.4 31.8 all-gather.5
  210.7 25.3 all-gather.7
  333.7 26.5 all-gather.9
